TPU v7x, 32 devices: a whole 2x2x4 slice. The times are simulated.
32 devices in a mesh: st: 4 (over x, core), fifth: 8 (over z, y).
Axes of the slice: x: 2, y: 2, z: 4, core: 2. Of those that a mesh axis runs over, the one named last changes fastest.
Arguments:
- source_field: float32 [2, 4, 3, 8, 4, 4096], P(None, None, None, 'fifth', 'st'), may hold values from -6 to 6
- gauge_rows: float32 [2, 4, 2, 3, 4, 4096], P(None, None, None, None, 'st', 'fifth'), may hold values from -3 to 3
Outputs:
- applied_once: float32 [2, 4, 3, 8, 4, 4096], P(None, None, None, 'fifth', 'st')
- applied_twice: float32 [2, 4, 3, 8, 4, 4096], P(None, None, None, 'fifth', 'st')
All inputs are finite; a program needn't handle non-finite values.
Results may differ from a plain program's by a relative error of at most 0.00002.
Values sent between devices are 32-bit elements; how exact they have to be, the bound alone decides.
A program may use at most 64 MiB of HBM per device.

v0:
```python
import functools

import jax
import jax.numpy as jnp
from jax import lax
from jax.experimental import pallas as pl
from jax.experimental.pallas import tpu as pltpu
from jax.sharding import PartitionSpec as P

WALL_HEIGHT = 1.8
QUARK_MASS = 0.5
MESH = pl.DeviceIdType.MESH
LANES = 128
ROWS = 8


def roll(value, shift, axis):
    return pltpu.roll(value, shift % value.shape[axis], axis)


def i_sigma(k, half):
    (r0, r1), (m0, m1) = half
    neg = lambda xs: [-x for x in xs]
    if k == 0:
        return [neg(m1), neg(m0)], [r1, r0]
    if k == 1:
        return [r1, neg(r0)], [m1, neg(m0)]
    return [neg(m0), m1], [r0, neg(r1)]


def combine(a, b, sign):
    op = (lambda x, y: x + y) if sign > 0 else (lambda x, y: x - y)
    return [[[op(x, y) for x, y in zip(sa, sb)] for sa, sb in zip(pa, pb)] for pa, pb in zip(a, b)]


def each(fn, *halves):
    return [
        [[fn(*xs) for xs in zip(*spins)] for spins in zip(*parts)] for parts in zip(*halves)
    ]


def colour_product(link, half, dagger):
    out = [[[None] * 3 for _ in range(2)] for _ in range(2)]
    for a in range(3):
        for b in range(3):
            re = link(0, b, a) if dagger else link(0, a, b)
            im = link(1, b, a) if dagger else link(1, a, b)
            for s in range(2):
                fr, fi = half[0][s][b], half[1][s][b]
                if dagger:
                    tr, ti = re * fr + im * fi, re * fi - im * fr
                else:
                    tr, ti = re * fr - im * fi, re * fi + im * fr
                out[0][s][a] = tr if b == 0 else out[0][s][a] + tr
                out[1][s][a] = ti if b == 0 else out[1][s][a] + ti
    return out


def kernel(n5, nt, rows, src, gauge, once, twice, gath, v_buf, part_buf, links, back, stage_in,
           stage_out, fifth_in, time_out, time_in, raw_in,
           gsend, grecv, lsem, fsend, frecv, tsend, trecv, rsend, rrecv, osem):
    me = lax.axis_index("fifth")
    mt = lax.axis_index("st")
    nxt, prv = lax.rem(me + 1, n5), lax.rem(me + n5 - 1, n5)
    t_nxt, t_prv = lax.rem(mt + 1, nt), lax.rem(mt + nt - 1, nt)
    q, m = me // 2, lax.rem(me, 2)
    nq = n5 // 2
    pair = q * 2 + 1 - m
    shard_rows = 48 * rows
    half_rows = 24 * rows

    load_src = pltpu.make_async_copy(src, stage_in, lsem.at[0])
    load_src.start()
    load_gauge = pltpu.make_async_copy(
        gauge, gath.at[pl.ds(pl.multiple_of(me * shard_rows, 8), shard_rows)], lsem.at[1]
    )
    load_gauge.start()

    barrier = pltpu.get_barrier_semaphore()
    for peer in (nxt, prv, lax.rem(me + 2, n5), lax.rem(me + n5 - 2, n5)):
        pl.semaphore_signal(barrier, inc=1, device_id={"fifth": peer}, device_id_type=MESH)
    for peer in (t_nxt, t_prv):
        pl.semaphore_signal(barrier, inc=1, device_id={"st": peer}, device_id_type=MESH)
    pl.semaphore_wait(barrier, 6)

    def shard(part, b):
        return gath.at[pl.ds(pl.multiple_of(b * shard_rows + part * half_rows, 8), half_rows)]

    def pass_on(part, b, kind, own=False):
        target = (me + 2, me - 2, pair)[kind]
        return pltpu.make_async_remote_copy(
            src_ref=gauge.at[pl.ds(part * half_rows, half_rows)] if own else shard(part, b),
            dst_ref=shard(part, b),
            send_sem=gsend.at[part, b, kind],
            recv_sem=grecv.at[part, b],
            device_id={"fifth": target},
            device_id_type=MESH,
        )

    def arrived(part, b):
        pass_on(part, b, 2).wait_recv()

    has_up, has_down = q + 1 < nq, q > 0

    pass_on(1, me, 2, True).start()
    pass_on(0, me, 2, True).start()

    @pl.when(has_up)
    def _():
        pass_on(0, me, 0, True).start()
        pass_on(1, me, 0, True).start()

    @pl.when(has_down)
    def _():
        pass_on(0, me, 1, True).start()
        pass_on(1, me, 1, True).start()

    def raw_copy(which):
        return pltpu.make_async_remote_copy(
            src_ref=src.at[:, pl.ds(6 * which, 6)],
            dst_ref=raw_in.at[which],
            send_sem=rsend.at[which],
            recv_sem=rrecv.at[which],
            device_id={"fifth": (nxt, prv)[which]},
            device_id_type=MESH,
        )

    raw_copy(0).start()
    raw_copy(1).start()

    def fifth_copy(which, j):
        return pltpu.make_async_remote_copy(
            src_ref=v_buf.at[1, j, :, pl.ds(6 * which, 6)],
            dst_ref=fifth_in.at[which, j],
            send_sem=fsend.at[which, j],
            recv_sem=frecv.at[which, j],
            device_id={"fifth": (nxt, prv)[which]},
            device_id_type=MESH,
        )

    def time_copy(phase, which, j):
        return pltpu.make_async_remote_copy(
            src_ref=time_out.at[phase, which, j],
            dst_ref=time_in.at[phase, which, j],
            send_sem=tsend.at[phase, which, j],
            recv_sem=trecv.at[phase, which, j],
            device_id={"st": (t_prv, t_nxt)[which]},
            device_id_type=MESH,
        )

    def load_half(ref, base):
        return [[[ref(p, base + 3 * s + c) for c in range(3)] for s in range(2)] for p in range(2)]

    def put_half(ref, half):
        for p in range(2):
            for s in range(2):
                for c in range(3):
                    ref[p, 3 * s + c] = half[p][s][c]

    load_src.wait()

    @pl.loop(0, 4)
    def _(j):
        for p in range(2):
            for c in range(12):
                v_buf[0, j, p, c] = stage_in[p, c, pl.ds(j, ROWS, stride=4), :]
        get = lambda p, c: v_buf[0, j, p, c]
        put_half(time_out.at[0, 0, j], combine(load_half(get, 0), load_half(get, 6), -1))
        time_copy(0, 0, j).start()

    arrived(1, pair)

    @pl.when(has_up)
    def _():
        pass_on(1, pair, 0).start()

    @pl.when(has_down)
    def _():
        pass_on(1, pair, 1).start()

    @pl.loop(1, nq)
    def _(k):
        below, above = me - 2 * k, me + 2 * k
        pair_below, pair_above = pair - 2 * k, pair + 2 * k

        @pl.when(q - k >= 0)
        def _():
            arrived(0, below)
            pass_on(0, below, 2).start()

            @pl.when(has_up)
            def _():
                pass_on(0, below, 0).start()

        @pl.when(q + k < nq)
        def _():
            arrived(0, above)
            pass_on(0, above, 2).start()

            @pl.when(has_down)
            def _():
                pass_on(0, above, 1).start()

        for b_low, b_high in ((below, above), (pair_below, pair_above)):

            @pl.when(q - k >= 0)
            def _():
                arrived(1, b_low)

                @pl.when(has_up)
                def _():
                    pass_on(1, b_low, 0).start()

            @pl.when(q + k < nq)
            def _():
                arrived(1, b_high)

                @pl.when(has_down)
                def _():
                    pass_on(1, b_high, 1).start()

    @pl.loop(0, nq)
    def _(k):
        arrived(0, 2 * k + 1 - m)

    load_gauge.wait()

    @pl.loop(0, 4)
    def _(j):
        offset = (j // rows) * shard_rows + lax.rem(j, rows)

        for mu in range(4):
            u = [[[None] * 3 for _ in range(3)] for _ in range(2)]
            for p in range(2):
                for a in range(2):
                    for b in range(3):
                        comp = ((p * 4 + mu) * 2 + a) * 3 + b
                        u[p][a][b] = gath[pl.ds(offset + comp * rows, ROWS, stride=192), :]
            (r0, r1, _), (m0, m1, _) = u
            for a in range(3):
                b, c = (a + 1) % 3, (a + 2) % 3
                u[0][2][a] = (r0[b] * r1[c] - m0[b] * m1[c]) - (r0[c] * r1[b] - m0[c] * m1[b])
                u[1][2][a] = (r0[c] * m1[b] + m0[c] * r1[b]) - (r0[b] * m1[c] + m0[b] * r1[c])
            for p in range(2):
                for a in range(3):
                    for b in range(3):
                        links[j, mu, p, 3 * a + b] = u[p][a][b]

    def time_link(j):
        return lambda p, a, b: links[j, 3, p, 3 * a + b]

    def send_behind(phase, j, get):
        total = combine(load_half(get, 0), load_half(get, 6), 1)
        put_half(time_out.at[phase, 1, j], colour_product(time_link(j), total, True))
        time_copy(phase, 1, j).start()

    @pl.loop(0, 4)
    def _(j):
        send_behind(0, j, lambda p, c: v_buf[0, j, p, c])

    lane = lax.broadcasted_iota(jnp.int32, (ROWS, LANES), 1)
    x = lax.rem(lane, 16)

    def xor1(j):
        return j + 1 - 2 * lax.rem(j, 2)

    def xor2(j):
        return lax.rem(j + 2, 4)

    def shift(k, ahead, j, here, there):
        if k == 0:
            if ahead:
                return jnp.where(x == 15, roll(here, 15, 1), roll(here, -1, 1))
            return jnp.where(x == 0, roll(here, -15, 1), roll(here, 1, 1))
        if k == 1:
            if ahead:
                return roll(jnp.where(lane >= 16, here, there), -16, 1)
            return roll(jnp.where(lane < LANES - 16, here, there), 16, 1)
        if ahead:
            return jnp.where(j >= 2, roll(there, -1, 0), there)
        return jnp.where(j < 2, roll(there, 1, 0), there)

    @pl.loop(0, 4)
    def _(j):
        other = (j, xor1(j), xor2(j))
        for k in range(3):
            for p in range(2):
                for c in range(9):
                    back[j, k, p, c] = shift(
                        k, False, j, links[j, k, p, c], links[other[k], k, p, c]
                    )

    time_last = jnp.where(mt == nt - 1, -1.0, 1.0).astype(jnp.float32)
    time_first = jnp.where(mt == 0, -1.0, 1.0).astype(jnp.float32)
    fifth_last = jnp.where(me == n5 - 1, -QUARK_MASS, 1.0).astype(jnp.float32)
    fifth_first = jnp.where(me == 0, -QUARK_MASS, 1.0).astype(jnp.float32)

    def local_part(phase):
        @pl.loop(0, 4)
        def _(j):
            other = (j, xor1(j), xor2(j))
            for k in range(3):

                def halves(at):
                    get = lambda p, c: v_buf[phase, at, p, c]
                    upper, turned = load_half(get, 0), i_sigma_lists(k, load_half(get, 6))
                    return combine(upper, turned, 1), combine(upper, turned, -1)

                there_plus, there_minus = halves(other[k])
                here_plus, here_minus = halves(j) if k == 1 else (there_plus, there_minus)
                go = lambda ahead: lambda h, t: shift(k, ahead, j, h, t)
                ahead_half = each(go(True), here_plus, there_plus)
                behind_half = each(go(False), here_minus, there_minus)
                moved_ahead = colour_product(
                    lambda p, a, b: links[j, k, p, 3 * a + b], ahead_half, False
                )
                moved_behind = colour_product(
                    lambda p, a, b: back[j, k, p, 3 * a + b], behind_half, True
                )
                upper = combine(moved_ahead, moved_behind, 1)
                lower = i_sigma_lists(k, combine(moved_behind, moved_ahead, -1))
                for base, half in ((0, upper), (6, lower)):
                    for p in range(2):
                        for s in range(2):
                            for c in range(3):
                                i = base + 3 * s + c
                                old = (
                                    (5.0 - WALL_HEIGHT) * v_buf[phase, j, p, i]
                                    if k == 0
                                    else part_buf[j, p, i]
                                )
                                part_buf[j, p, i] = old - 0.5 * half[p][s][c]

    def finish(phase):
        @pl.loop(0, 4)
        def _(j):
            time_copy(phase, 0, j).wait_recv()
            time_copy(phase, 1, j).wait_recv()
            if phase == 1:
                fifth_copy(0, j).wait_recv()
                fifth_copy(1, j).wait_recv()
            ahead = load_half(lambda p, c: time_in[phase, 0, j, p, c] * time_last, 0)
            behind = load_half(lambda p, c: time_in[phase, 1, j, p, c] * time_first, 0)
            moved = colour_product(time_link(j), ahead, False)
            upper = combine(moved, behind, 1)
            lower = combine(behind, moved, -1)
            for which, half in ((0, upper), (1, lower)):
                for p in range(2):
                    for s in range(2):
                        for c in range(3):
                            i = 3 * s + c
                            if phase == 0:
                                chiral = raw_in[which, p, i, pl.ds(j, ROWS, stride=4), :]
                            else:
                                chiral = fifth_in[which, j, p, i]
                            chiral = chiral * (fifth_first, fifth_last)[which]
                            value = part_buf[j, p, 6 * which + i] - 0.5 * half[p][s][c] - chiral
                            stage_out[phase, p, 6 * which + i, pl.ds(j, ROWS, stride=4), :] = value
                            if phase == 0:
                                v_buf[1, j, p, 6 * which + i] = value
            if phase == 0:
                fifth_copy(0, j).start()
                fifth_copy(1, j).start()
                get = lambda p, c: v_buf[1, j, p, c]
                put_half(time_out.at[1, 0, j], combine(load_half(get, 0), load_half(get, 6), -1))
                time_copy(1, 0, j).start()
                send_behind(1, j, get)

    local_part(0)
    raw_copy(0).wait_recv()
    raw_copy(1).wait_recv()
    finish(0)
    write_once = pltpu.make_async_copy(stage_out.at[0], once, osem.at[0])
    write_once.start()
    local_part(1)
    finish(1)
    write_twice = pltpu.make_async_copy(stage_out.at[1], twice, osem.at[1])
    write_twice.start()

    raw_copy(0).wait_send()
    raw_copy(1).wait_send()

    @pl.loop(0, 4)
    def _(j):
        for which in range(2):
            fifth_copy(which, j).wait_send()
            time_copy(0, which, j).wait_send()
            time_copy(1, which, j).wait_send()

    for b in (me, pair):

        @pl.when(has_up)
        def _():
            pass_on(1, b, 0).wait_send()

        @pl.when(has_down)
        def _():
            pass_on(1, b, 1).wait_send()

    pass_on(1, me, 2).wait_send()
    pass_on(0, me, 2).wait_send()

    @pl.when(has_up)
    def _():
        pass_on(0, me, 0).wait_send()

    @pl.when(has_down)
    def _():
        pass_on(0, me, 1).wait_send()

    @pl.loop(1, nq)
    def _(k):
        below, above = me - 2 * k, me + 2 * k
        pair_below, pair_above = pair - 2 * k, pair + 2 * k

        @pl.when(q - k >= 0)
        def _():
            pass_on(0, below, 2).wait_send()

            @pl.when(has_up)
            def _():
                pass_on(0, below, 0).wait_send()
                pass_on(1, below, 0).wait_send()
                pass_on(1, pair_below, 0).wait_send()

        @pl.when(q + k < nq)
        def _():
            pass_on(0, above, 2).wait_send()

            @pl.when(has_down)
            def _():
                pass_on(0, above, 1).wait_send()
                pass_on(1, above, 1).wait_send()
                pass_on(1, pair_above, 1).wait_send()

    write_once.wait()
    write_twice.wait()


def i_sigma_lists(k, half):
    return [list(part) for part in i_sigma(k, half)]


def on_device(n5, nt, source_field, gauge_rows):
    rows = gauge_rows.shape[-1] // LANES
    src = source_field.reshape(2, 12, 32, LANES)
    gauge = gauge_rows.reshape(48 * rows, LANES)
    field = jax.ShapeDtypeStruct((2, 12, 32, LANES), jnp.float32)
    f32 = lambda *shape: pltpu.VMEM(shape, jnp.float32)
    sem = lambda *shape: pltpu.SemaphoreType.DMA(shape)
    once, twice = pl.pallas_call(
        functools.partial(kernel, n5, nt, rows),
        out_shape=(field, field),
        in_specs=[pl.BlockSpec(memory_space=pl.ANY)] * 2,
        out_specs=[pl.BlockSpec(memory_space=pl.ANY)] * 2,
        scratch_shapes=[
            f32(n5 * 48 * rows, LANES),
            f32(2, 4, 2, 12, ROWS, LANES),
            f32(4, 2, 12, ROWS, LANES),
            f32(4, 4, 2, 9, ROWS, LANES),
            f32(4, 3, 2, 9, ROWS, LANES),
            f32(2, 12, 32, LANES),
            f32(2, 2, 12, 32, LANES),
            f32(2, 4, 2, 6, ROWS, LANES),
            f32(2, 2, 4, 2, 6, ROWS, LANES),
            f32(2, 2, 4, 2, 6, ROWS, LANES),
            f32(2, 2, 6, 32, LANES),
            sem(2, n5, 3),
            sem(2, n5),
            sem(2),
            sem(2, 4),
            sem(2, 4),
            sem(2, 2, 4),
            sem(2, 2, 4),
            sem(2),
            sem(2),
            sem(2),
        ],
        compiler_params=pltpu.CompilerParams(
            collective_id=0, has_side_effects=True, vmem_limit_bytes=40 * 1024 * 1024
        ),
    )(src, gauge)
    return once.reshape(source_field.shape), twice.reshape(source_field.shape)


def solution(mesh):
    spec = P(None, None, None, "fifth", "st", None)
    return jax.shard_map(
        functools.partial(on_device, mesh.shape["fifth"], mesh.shape["st"]),
        mesh=mesh,
        in_specs=(spec, P(None, None, None, None, "st", "fifth")),
        out_specs=(spec, spec),
        check_vma=False,
    )
```

profile of v0, /device:TPU:0, one launch (start us, length us, event | category | flops | bytes accessed | tf_op | source)
XLA Modules:
  0.0 40.1 jit_solution(14047854808597133682)
XLA Ops:
  0.6 0.0 copy-start
  0.6 1.0 %copy-done = f32[2,4,3,1,1,4096]{5,4,3,2,1,0:T(1,128)S(1)} copy-done((f32[2,4,3,1,1,4096]{5,4,3,2,1,0:T(1,128)S(1)}, f32[2,4,3,1,1,4096]{5,4,3,2,1,0:T(1,128)}, u32[]{:S(2)}) %copy-start) | copy-done | bytes 393240
  1.6 0.0 copy-start.1
  1.6 0.9 %copy-done.1 = f32[2,4,2,3,1,512]{5,4,3,2,1,0:T(1,128)S(1)} copy-done((f32[2,4,2,3,1,512]{5,4,3,2,1,0:T(1,128)S(1)}, f32[2,4,2,3,1,512]{5,4,3,2,1,0:T(1,128)}, u32[]{:S(2)}) %copy-start.1) | copy-done | bytes 98328
  2.5 36.0 %shard_map.41 = (f32[2,12,32,128]{3,2,1,0:T(8,128)S(1)}, f32[2,12,32,128]{3,2,1,0:T(8,128)S(1)}) custom-call(f32[2,12,32,128]{3,2,1,0:T(8,128)S(1)} %bitcast.6, f32[192,128]{1,0:T(8,128)S(1)} %bitcast.7), custom_call_target="tpu_custom_call" | custom-call | tf_op jit(solution)/shard_map/pallas_call | solution.py:451
  38.6 0.7 %copy.16 = f32[2,4,3,1,1,4096]{5,4,3,2,1,0:T(1,128)} copy(f32[2,4,3,1,1,4096]{5,4,3,2,1,0:T(1,128)S(1)} %bitcast.5) | data formatting | bytes 786432
  39.3 0.7 %copy.17 = f32[2,4,3,1,1,4096]{5,4,3,2,1,0:T(1,128)} copy(f32[2,4,3,1,1,4096]{5,4,3,2,1,0:T(1,128)S(1)} %bitcast.4) | data formatting | bytes 786432
Async XLA Ops:
  0.6 1.0 %copy-start = (f32[2,4,3,1,1,4096]{5,4,3,2,1,0:T(1,128)S(1)}, f32[2,4,3,1,1,4096]{5,4,3,2,1,0:T(1,128)}, u32[]{:S(2)}) copy-start(f32[2,4,3,1,1,4096]{5,4,3,2,1,0:T(1,128)} %param.2) | copy-start | bytes 1179652
  1.6 0.9 %copy-start.1 = (f32[2,4,2,3,1,512]{5,4,3,2,1,0:T(1,128)S(1)}, f32[2,4,2,3,1,512]{5,4,3,2,1,0:T(1,128)}, u32[]{:S(2)}) copy-start(f32[2,4,2,3,1,512]{5,4,3,2,1,0:T(1,128)} %param.3) | copy-start | bytes 294916
where the time goes:
time: 40.2 us; the launch traced here: 40.1 us
  Pallas kernels  36 us (90%)
  local copies, waits for them, and re-layouts  3.37 us (8%)
  between operations  0.65 us (2%)
    pallas_call x1, Pallas kernels, on_device(): pl.pallas_call(functools.partial(kernel, n5, nt, rows), out_shape=(field,...  36 us
    unnamed x6, local copies, waits for them, and re-layouts  3.37 us

commit v1 on v0

--- a/solution.py
+++ b/solution.py
@@ -56,9 +56,9 @@
     return out
 
 
-def kernel(n5, nt, rows, src, gauge, once, twice, gath, v_buf, part_buf, links, back, stage_in,
+def kernel(n5, nt, rows, src, gauge, once, twice, gath, gath_back, v_buf, part_buf, links, back, stage_in,
            stage_out, fifth_in, time_out, time_in, raw_in,
-           gsend, grecv, lsem, fsend, frecv, tsend, trecv, rsend, rrecv, osem):
+           gsend, grecv, bsend, brecv, lsem, fsend, frecv, tsend, trecv, rsend, rrecv, osem):
     me = lax.axis_index("fifth")
     mt = lax.axis_index("st")
     nxt, prv = lax.rem(me + 1, n5), lax.rem(me + n5 - 1, n5)
@@ -97,6 +97,20 @@
             device_id_type=MESH,
         )
 
+    time_rows = -(-6 * rows // 8) * 8
+
+    def time_rows_on(part, b, own=False):
+        first = part * half_rows + half_rows - time_rows
+        span = pl.ds(pl.multiple_of(b * shard_rows + first, 8), time_rows)
+        return pltpu.make_async_remote_copy(
+            src_ref=gauge.at[pl.ds(first, time_rows)] if own else gath.at[span],
+            dst_ref=gath_back.at[span],
+            send_sem=bsend.at[part, b],
+            recv_sem=brecv.at[part, b],
+            device_id={"st": t_nxt},
+            device_id_type=MESH,
+        )
+
     def arrived(part, b):
         pass_on(part, b, 2).wait_recv()
 
@@ -114,6 +128,9 @@
     def _():
         pass_on(0, me, 1, True).start()
         pass_on(1, me, 1, True).start()
+
+    time_rows_on(0, me, True).start()
+    time_rows_on(1, me, True).start()
 
     def raw_copy(which):
         return pltpu.make_async_remote_copy(
@@ -166,7 +183,9 @@
                 v_buf[0, j, p, c] = stage_in[p, c, pl.ds(j, ROWS, stride=4), :]
         get = lambda p, c: v_buf[0, j, p, c]
         put_half(time_out.at[0, 0, j], combine(load_half(get, 0), load_half(get, 6), -1))
+        put_half(time_out.at[0, 1, j], combine(load_half(get, 0), load_half(get, 6), 1))
         time_copy(0, 0, j).start()
+        time_copy(0, 1, j).start()
 
     arrived(1, pair)
 
@@ -177,6 +196,8 @@
     @pl.when(has_down)
     def _():
         pass_on(1, pair, 1).start()
+
+    time_rows_on(1, pair).start()
 
     @pl.loop(1, nq)
     def _(k):
@@ -186,21 +207,25 @@
         @pl.when(q - k >= 0)
         def _():
             arrived(0, below)
-            pass_on(0, below, 2).start()
 
             @pl.when(has_up)
             def _():
                 pass_on(0, below, 0).start()
 
+            pass_on(0, below, 2).start()
+            time_rows_on(0, below).start()
+
         @pl.when(q + k < nq)
         def _():
             arrived(0, above)
-            pass_on(0, above, 2).start()
 
             @pl.when(has_down)
             def _():
                 pass_on(0, above, 1).start()
 
+            pass_on(0, above, 2).start()
+            time_rows_on(0, above).start()
+
         for b_low, b_high in ((below, above), (pair_below, pair_above)):
 
             @pl.when(q - k >= 0)
@@ -211,6 +236,8 @@
                 def _():
                     pass_on(1, b_low, 0).start()
 
+                time_rows_on(1, b_low).start()
+
             @pl.when(q + k < nq)
             def _():
                 arrived(1, b_high)
@@ -219,44 +246,37 @@
                 def _():
                     pass_on(1, b_high, 1).start()
 
+                time_rows_on(1, b_high).start()
+
     @pl.loop(0, nq)
     def _(k):
         arrived(0, 2 * k + 1 - m)
+        time_rows_on(0, 2 * k + 1 - m).start()
 
     load_gauge.wait()
+
+    def complete(source, j, mu, slot):
+        offset = (j // rows) * shard_rows + lax.rem(j, rows)
+        u = [[[None] * 3 for _ in range(3)] for _ in range(2)]
+        for p in range(2):
+            for a in range(2):
+                for b in range(3):
+                    comp = ((p * 4 + mu) * 2 + a) * 3 + b
+                    u[p][a][b] = source[pl.ds(offset + comp * rows, ROWS, stride=192), :]
+        (r0, r1, _), (m0, m1, _) = u
+        for a in range(3):
+            b, c = (a + 1) % 3, (a + 2) % 3
+            u[0][2][a] = (r0[b] * r1[c] - m0[b] * m1[c]) - (r0[c] * r1[b] - m0[c] * m1[b])
+            u[1][2][a] = (r0[c] * m1[b] + m0[c] * r1[b]) - (r0[b] * m1[c] + m0[b] * r1[c])
+        for p in range(2):
+            for a in range(3):
+                for b in range(3):
+                    links[j, slot, p, 3 * a + b] = u[p][a][b]
 
     @pl.loop(0, 4)
     def _(j):
-        offset = (j // rows) * shard_rows + lax.rem(j, rows)
-
         for mu in range(4):
-            u = [[[None] * 3 for _ in range(3)] for _ in range(2)]
-            for p in range(2):
-                for a in range(2):
-                    for b in range(3):
-                        comp = ((p * 4 + mu) * 2 + a) * 3 + b
-                        u[p][a][b] = gath[pl.ds(offset + comp * rows, ROWS, stride=192), :]
-            (r0, r1, _), (m0, m1, _) = u
-            for a in range(3):
-                b, c = (a + 1) % 3, (a + 2) % 3
-                u[0][2][a] = (r0[b] * r1[c] - m0[b] * m1[c]) - (r0[c] * r1[b] - m0[c] * m1[b])
-                u[1][2][a] = (r0[c] * m1[b] + m0[c] * r1[b]) - (r0[b] * m1[c] + m0[b] * r1[c])
-            for p in range(2):
-                for a in range(3):
-                    for b in range(3):
-                        links[j, mu, p, 3 * a + b] = u[p][a][b]
-
-    def time_link(j):
-        return lambda p, a, b: links[j, 3, p, 3 * a + b]
-
-    def send_behind(phase, j, get):
-        total = combine(load_half(get, 0), load_half(get, 6), 1)
-        put_half(time_out.at[phase, 1, j], colour_product(time_link(j), total, True))
-        time_copy(phase, 1, j).start()
-
-    @pl.loop(0, 4)
-    def _(j):
-        send_behind(0, j, lambda p, c: v_buf[0, j, p, c])
+            complete(gath, j, mu, mu)
 
     lane = lax.broadcasted_iota(jnp.int32, (ROWS, LANES), 1)
     x = lax.rem(lane, 16)
@@ -341,7 +361,8 @@
                 fifth_copy(1, j).wait_recv()
             ahead = load_half(lambda p, c: time_in[phase, 0, j, p, c] * time_last, 0)
             behind = load_half(lambda p, c: time_in[phase, 1, j, p, c] * time_first, 0)
-            moved = colour_product(time_link(j), ahead, False)
+            moved = colour_product(lambda p, a, b: links[j, 3, p, 3 * a + b], ahead, False)
+            behind = colour_product(lambda p, a, b: links[j, 4, p, 3 * a + b], behind, True)
             upper = combine(moved, behind, 1)
             lower = combine(behind, moved, -1)
             for which, half in ((0, upper), (1, lower)):
@@ -364,9 +385,20 @@
                 get = lambda p, c: v_buf[1, j, p, c]
                 put_half(time_out.at[1, 0, j], combine(load_half(get, 0), load_half(get, 6), -1))
                 time_copy(1, 0, j).start()
-                send_behind(1, j, get)
+                put_half(time_out.at[1, 1, j], combine(load_half(get, 0), load_half(get, 6), 1))
+                time_copy(1, 1, j).start()
 
     local_part(0)
+
+    @pl.loop(0, n5)
+    def _(b):
+        time_rows_on(0, b).wait_recv()
+        time_rows_on(1, b).wait_recv()
+
+    @pl.loop(0, 4)
+    def _(j):
+        complete(gath_back, j, 3, 4)
+
     raw_copy(0).wait_recv()
     raw_copy(1).wait_recv()
     finish(0)
@@ -386,6 +418,11 @@
             fifth_copy(which, j).wait_send()
             time_copy(0, which, j).wait_send()
             time_copy(1, which, j).wait_send()
+
+    @pl.loop(0, n5)
+    def _(b):
+        time_rows_on(0, b).wait_send()
+        time_rows_on(1, b).wait_send()
 
     for b in (me, pair):
 
@@ -455,9 +492,10 @@
         out_specs=[pl.BlockSpec(memory_space=pl.ANY)] * 2,
         scratch_shapes=[
             f32(n5 * 48 * rows, LANES),
+            f32(n5 * 48 * rows, LANES),
             f32(2, 4, 2, 12, ROWS, LANES),
             f32(4, 2, 12, ROWS, LANES),
-            f32(4, 4, 2, 9, ROWS, LANES),
+            f32(4, 5, 2, 9, ROWS, LANES),
             f32(4, 3, 2, 9, ROWS, LANES),
             f32(2, 12, 32, LANES),
             f32(2, 2, 12, 32, LANES),
@@ -466,6 +504,8 @@
             f32(2, 2, 4, 2, 6, ROWS, LANES),
             f32(2, 2, 6, 32, LANES),
             sem(2, n5, 3),
+            sem(2, n5),
+            sem(2, n5),
             sem(2, n5),
             sem(2),
             sem(2, 4),
@@ -477,7 +517,7 @@
             sem(2),
         ],
         compiler_params=pltpu.CompilerParams(
-            collective_id=0, has_side_effects=True, vmem_limit_bytes=40 * 1024 * 1024
+            collective_id=0, has_side_effects=True, vmem_limit_bytes=66187264
         ),
     )(src, gauge)
     return once.reshape(source_field.shape), twice.reshape(source_field.shape)

time: 40.2 us -> 39.7 us (0.988)
  local copies, waits for them, and re-layouts: 3.37 us -> 2.57 us
    unnamed x6 -> x4, local copies, waits for them, and re-layouts: 3.37 us -> 2.57 us
where the time goes in v1:
time: 39.7 us; the launch traced here: 39.5 us
  Pallas kernels  36.3 us (91%)
  local copies, waits for them, and re-layouts  2.57 us (6%)
  between operations  0.65 us (2%)
    pallas_call x1, Pallas kernels, on_device(): pl.pallas_call(functools.partial(kernel, n5, nt, rows), out_shape=(field,...  36.3 us
    unnamed x4, local copies, waits for them, and re-layouts  2.57 us

profile of v1, /device:TPU:0, one launch (start us, length us, event | category | flops | bytes accessed | tf_op | source)
XLA Modules:
  0.0 39.5 jit_solution(12425402756029276047)
XLA Ops:
  0.6 36.3 %shard_map.41 = (f32[2,12,32,128]{3,2,1,0:T(8,128)}, f32[2,12,32,128]{3,2,1,0:T(8,128)}) custom-call(f32[2,12,32,128]{3,2,1,0:T(8,128)} %bitcast.6, f32[192,128]{1,0:T(8,128)} %bitcast.7), custom_call_target="tpu_custom_call" | custom-call | tf_op jit(solution)/shard_map/pallas_call | solution.py:488
  37.0 0.0 copy-start
  37.0 1.8 %copy.16 = f32[2,4,3,1,1,4096]{5,4,3,2,1,0:T(1,128)} copy(f32[2,4,3,1,1,4096]{5,4,3,2,1,0:T(1,128)} %bitcast.5) | data formatting | bytes 786432
  38.8 0.0 copy-done
  38.8 0.7 %copy.17 = f32[2,4,3,1,1,4096]{5,4,3,2,1,0:T(1,128)} copy(f32[2,4,3,1,1,4096]{5,4,3,2,1,0:T(1,128)S(1)} %bitcast.4) | data formatting | bytes 786432
Async XLA Ops:
  37.0 1.8 %copy-start = (f32[2,12,32,128]{3,2,1,0:T(8,128)S(1)}, f32[2,12,32,128]{3,2,1,0:T(8,128)}, u32[]{:S(2)}) copy-start(f32[2,12,32,128]{3,2,1,0:T(8,128)} %get-tuple-element.5) | copy-start | bytes 1179652

commit v2 on v1

--- a/solution.py
+++ b/solution.py
@@ -379,9 +379,9 @@
                             stage_out[phase, p, 6 * which + i, pl.ds(j, ROWS, stride=4), :] = value
                             if phase == 0:
                                 v_buf[1, j, p, 6 * which + i] = value
+                if phase == 0:
+                    fifth_copy(which, j).start()
             if phase == 0:
-                fifth_copy(0, j).start()
-                fifth_copy(1, j).start()
                 get = lambda p, c: v_buf[1, j, p, c]
                 put_half(time_out.at[1, 0, j], combine(load_half(get, 0), load_half(get, 6), -1))
                 time_copy(1, 0, j).start()

time: 39.7 us -> 39.7 us (level)
  no operation moved by 1% of the time
where the time goes in v2:
time: 39.7 us; the launch traced here: 39.5 us
  Pallas kernels  36.3 us (91%)
  local copies, waits for them, and re-layouts  2.57 us (6%)
  between operations  0.65 us (2%)
    pallas_call x1, Pallas kernels, on_device(): pl.pallas_call(functools.partial(kernel, n5, nt, rows), out_shape=(field,...  36.3 us
    unnamed x4, local copies, waits for them, and re-layouts  2.57 us

profile of v2, /device:TPU:0, one launch (start us, length us, event | category | flops | bytes accessed | tf_op | source)
XLA Modules:
  0.0 39.5 jit_solution(16707046342238521791)
XLA Ops:
  0.6 36.3 %shard_map.41 = (f32[2,12,32,128]{3,2,1,0:T(8,128)}, f32[2,12,32,128]{3,2,1,0:T(8,128)}) custom-call(f32[2,12,32,128]{3,2,1,0:T(8,128)} %bitcast.6, f32[192,128]{1,0:T(8,128)} %bitcast.7), custom_call_target="tpu_custom_call" | custom-call | tf_op jit(solution)/shard_map/pallas_call | solution.py:488
  37.0 0.0 copy-start
  37.0 1.8 %copy.16 = f32[2,4,3,1,1,4096]{5,4,3,2,1,0:T(1,128)} copy(f32[2,4,3,1,1,4096]{5,4,3,2,1,0:T(1,128)} %bitcast.5) | data formatting | bytes 786432
  38.8 0.0 copy-done
  38.8 0.7 %copy.17 = f32[2,4,3,1,1,4096]{5,4,3,2,1,0:T(1,128)} copy(f32[2,4,3,1,1,4096]{5,4,3,2,1,0:T(1,128)S(1)} %bitcast.4) | data formatting | bytes 786432
Async XLA Ops:
  37.0 1.8 %copy-start = (f32[2,12,32,128]{3,2,1,0:T(8,128)S(1)}, f32[2,12,32,128]{3,2,1,0:T(8,128)}, u32[]{:S(2)}) copy-start(f32[2,12,32,128]{3,2,1,0:T(8,128)} %get-tuple-element.5) | copy-start | bytes 1179652
